TPU v7x, 256 devices: a whole 4x4x8 slice. The times are simulated.
256 devices in a mesh: ex: 64 (over y, z, core), rep: 4 (over x).
Axes of the slice: x: 4, y: 4, z: 8, core: 2. Of those that a mesh axis runs over, the one named last changes fastest.
Arguments:
- embeddings: bfloat16 [393216, 1024], P(('ex', 'rep')), may hold values from -6 to 6
- block_rows: bfloat16 [98304, 1024], P(('ex', 'rep')), may hold values from -6 to 6
- owners: int32 [98304, 1], P(('ex', 'rep')), may hold values from 0 to 63; in each aligned block of 384 rows (0 to 383, 384 to 767, ...) at most 12 rows name the same one
- query_cluster: int32 [98304], P(('ex', 'rep')), may hold values from 0 to 7
- member_cluster: int32 [64, 6144], P('ex', 'rep'), may hold values from 0 to 7, never falling along the last dimension, each value on 1 to 1536 neighbouring positions
Outputs:
- query_max: float32 [98304], P(('ex', 'rep'))
- resident_max: float32 [393216], P(('ex', 'rep'))
Inputs may be any that keep to these rules, and one draw needn't show every extreme that they name: `owners`: among the rows of one device each group is named by at most 12 rows, a bound that some block reaches. `member_cluster`: nondecreasing along each group's row; each of the 8 clusters has at least one member in every group.
All inputs are finite; a program needn't handle non-finite values.
Results may differ from a plain program's by a relative error of at most 0.0016.
Values may be sent and summed in bfloat16 or wider, within the bound.
A program may use at most 64 MiB of HBM per device.

v0:
```python
import jax
import jax.numpy as jnp
from jax import lax
from jax.sharding import PartitionSpec as P


def unit_length(matrix):
    wide = matrix.astype(jnp.float32)
    squares = jnp.sum(wide * wide, axis=1, keepdims=True)
    return (wide * lax.rsqrt(squares + 1e-06)).astype(jnp.bfloat16)


def tile_scores(query_part, query_labels, member_part, member_labels):
    cosines = lax.dot_general(
        query_part, member_part, (((1,), (1,)), ((), ())), preferred_element_type=jnp.float32
    )
    same_cluster = query_labels[:, None] == member_labels[None, :]
    return jnp.where(same_cluster, cosines, -1.0)


def shards(embeddings, block_rows, owners, query_cluster, member_cluster):
    ex_count = lax.axis_size("ex")
    rep_index = lax.axis_index("rep")
    slot_count = 2 * block_rows.shape[0]
    capacity = slot_count // ex_count
    member_count = embeddings.shape[0]
    members = unit_length(embeddings)
    queries = unit_length(block_rows)
    targets = owners[:, 0]
    one_hot = (targets[:, None] == jnp.arange(ex_count, dtype=jnp.int32)[None, :]).astype(jnp.int32)
    before = jnp.cumsum(one_hot, axis=0) - one_hot
    slots = targets * capacity + jnp.sum(before * one_hot, axis=1)
    outgoing = jnp.zeros((slot_count, queries.shape[1]), jnp.bfloat16).at[slots].set(queries)
    out_labels = (
        jnp.zeros((slot_count,), jnp.bfloat16)
        .at[slots]
        .set((query_cluster + 1).astype(jnp.bfloat16))
    )
    arrived, arrived_labels = (
        lax.all_to_all(outgoing, "ex", split_axis=0, concat_axis=0, tiled=True),
        lax.all_to_all(out_labels, "ex", split_axis=0, concat_axis=0, tiled=True),
    )
    member_labels = (member_cluster[0] + 1).astype(jnp.bfloat16)
    start_columns = jnp.full((member_count,), -1.0, jnp.float32)
    scores = tile_scores(
        lax.all_gather(arrived, "rep", axis=0, tiled=True),
        lax.all_gather(arrived_labels, "rep", axis=0, tiled=True),
        members,
        member_labels,
    )
    row_all = jnp.max(scores, axis=1)
    row_all, resident_max = (row_all, jnp.maximum(start_columns, jnp.max(scores, axis=0)))
    row_all = lax.pmax(row_all, "rep")
    row_best = lax.dynamic_slice_in_dim(row_all, rep_index * slot_count, slot_count, 0)
    returned = lax.all_to_all(row_best, "ex", split_axis=0, concat_axis=0, tiled=True)
    query_max = returned[slots]
    return (query_max, resident_max)


def solution(mesh):
    placed = (
        P(("ex", "rep"), None),
        P(("ex", "rep"), None),
        P(("ex", "rep"), None),
        P(("ex", "rep")),
        P("ex", "rep"),
    )
    return jax.shard_map(
        shards,
        mesh=mesh,
        in_specs=placed,
        out_specs=(P(("ex", "rep")), P(("ex", "rep"))),
        check_vma=False,
    )
```

profile of v0, /device:TPU:1, one launch (start us, length us, event | category | flops | bytes accessed | tf_op | source)
XLA Modules:
  0.0 211.7 jit_solution(8776450861866258168)
XLA Ops:
  7.2 0.7 reduce
  7.9 0.9 reduce-window.6
  9.2 0.7 fusion.17
  9.9 1.4 fusion.7
  11.3 4.0 %scatter_custom_fusion.1 = bf16[768,1024]{1,0:T(8,128)(2,1)} fusion(s32[384]{0:T(512)S(1)} %fusion.17, bf16[384,1024]{1,0:T(8,128)(2,1)} %param.6, f32[384]{0:T(512)S(1)} %add_rsqrt_fusion.1, bf16[]{:T(256)} %constant.11.clone.1), kind=kCustom, calls=%fused_computation.16 | custom fusion | flops 1179648 | bytes 2361346 | tf_op jit(solution)/shard_map/scatter | solution.py:33
  15.3 2.4 %all_to_all.27 = bf16[64,12,1024]{2,1,0:T(8,128)(2,1)S(1)} reshape(bf16[768,1024]{1,0:T(8,128)(2,1)} %scatter_custom_fusion.1) | data formatting | bytes 3145728 | tf_op jit(solution)/shard_map/all_to_all | solution.py:40
  17.7 64.3 %all_to_all.37 = bf16[64,12,1024]{2,1,0:T(8,128)(2,1)} all-to-all(bf16[64,12,1024]{2,1,0:T(8,128)(2,1)S(1)} %all_to_all.27), channel_id=1, replica_groups=mesh['ex'=64,'rep'=4] {'ex'}, dimensions={0} | all-to-all | bytes 3145728 | tf_op jit(solution)/shard_map/all_to_all | solution.py:40
  82.0 3.8 %all_to_all.29 = bf16[768,1024]{1,0:T(8,128)(2,1)} reshape(bf16[64,12,1024]{2,1,0:T(8,128)(2,1)} %all_to_all.37) | data formatting | bytes 3145728 | tf_op jit(solution)/shard_map/all_to_all | solution.py:40
  85.8 3.0 %scatter_custom_fusion = bf16[768]{0:T(1024)(128)(2,1)S(1)} fusion(s32[384]{0:T(512)S(1)} %fusion.17, bf16[384]{0:T(512)(128)(2,1)S(1)} %add_convert_fusion, bf16[]{:T(256)} %constant.11.clone.1), kind=kCustom, calls=%fused_computation.36 | custom fusion | bytes 1538 | tf_op jit(solution)/shard_map/scatter | solution.py:37
  88.8 0.7 all_to_all.33
  89.5 5.8 %all-to-all-start = ((bf16[64,12,1]{1,2,0:T(2,128)(2,1)}), bf16[64,12,1]{1,2,0:T(2,128)(2,1)S(1)}, u32[]{:S(2)}, u32[]{:S(2)}) async-start(bf16[64,12,1]{1,2,0:T(2,128)(2,1)} %all_to_all.33), calls=%async_computation | async-start | bytes 65536 | tf_op jit(solution)/shard_map/all_to_all | solution.py:41
  95.4 0.7 fusion.2
  96.1 8.5 %all-to-all-done = bf16[64,12,1]{1,2,0:T(2,128)(2,1)S(1)} async-done(((bf16[64,12,1]{1,2,0:T(2,128)(2,1)}), bf16[64,12,1]{1,2,0:T(2,128)(2,1)S(1)}, u32[]{:S(2)}, u32[]{:S(2)}) %all-to-all-start) | async-done | bytes 1568 | tf_op jit(solution)/shard_map/all_to_all | solution.py:41
  104.8 10.5 %all-gather = bf16[4,1,768]{2,1,0:T(2,128)(2,1)S(1)} all-gather(bf16[1,1,768]{2,1,0:T(2,128)(2,1)S(1)} %reshape.65), channel_id=1, replica_groups=mesh['ex'=64,'rep'=4] {'rep'}, dimensions={0}, use_global_device_ids=true | all-gather | bytes 7680 | tf_op jit(solution)/shard_map/all_gather | solution.py:47
  115.4 35.3 %all-gather.3.cloned.1.call-done = bf16[3072,1024]{1,0:T(8,128)(2,1)} async-done(((bf16[768,1024]{1,0:T(8,128)(2,1)}), bf16[3072,1024]{1,0:T(8,128)(2,1)}) %all-gather.3.cloned.1.call-update) | async-done | bytes 6291472 | tf_op jit(solution)/shard_map/all_gather | solution.py:46
  150.7 13.4 %fusion = (f32[1536]{0:T(1024)S(1)}, f32[3072]{0:T(1024)S(1)}) fusion(bf16[1536]{0:T(1024)(128)(2,1)S(1)} %convert_reduce_fusion, bf16[3072]{0:T(1024)(128)(2,1)S(1)} %reshape.66, bf16[3072,1024]{1,0:T(8,128)(2,1)} %all-gather.3.cloned.1.call-done, bf16[1536,1024]{1,0:T(8,128)(2,1)S(1)} %copy-done, f32[1536]{0:T(1024)S(1)} %add_rsqrt_fusion), kind=kOutput, calls=%fused_computation.4 | convolution fusion | flops 9687264256 | bytes 9470976 | tf_op jit(solution)/shard_map/dot_general | solution.py:14
  164.2 11.6 %pmax.7 = f32[3072]{0:T(1024)S(1)} all-reduce(f32[3072]{0:T(1024)S(1)} %get-tuple-element.3), channel_id=1, replica_groups=mesh['ex'=64,'rep'=4] {'rep'}, use_global_device_ids=true, to_apply=%region_8.9 | all-reduce | flops 3072 | bytes 24576 | tf_op jit(solution)/shard_map/pmax | solution.py:53
  175.9 0.7 all_to_all.30
  176.6 14.6 %all-to-all-start.2 = ((f32[64,12,1]{1,2,0:T(1,128)}), f32[64,12,1]{1,2,0:T(1,128)S(1)}, u32[]{:S(2)}, u32[]{:S(2)}) async-start(f32[64,12,1]{1,2,0:T(1,128)} %bitcast.1), calls=%async_computation.2 | async-start | bytes 65536 | tf_op jit(solution)/shard_map/all_to_all | solution.py:55
  191.2 0.6 broadcast_maximum_fusion
  191.8 8.7 %all-to-all-done.2 = f32[64,12,1]{1,2,0:T(1,128)S(1)} async-done(((f32[64,12,1]{1,2,0:T(1,128)}), f32[64,12,1]{1,2,0:T(1,128)S(1)}, u32[]{:S(2)}, u32[]{:S(2)}) %all-to-all-start.2) | async-done | bytes 3104 | tf_op jit(solution)/shard_map/all_to_all | solution.py:55
  200.5 0.5 broadcast.57
  201.0 0.7 reduce.13
  201.8 3.0 %gather_fusion = f32[384]{0:T(512)} fusion(f32[768]{0:T(1024)S(1)} %all_to_all.32, s32[1024]{0:T(1024)S(1)} %pad_clamp_fusion), kind=kCustom, calls=%fused_computation | custom fusion | bytes 4608 | tf_op jit(solution)/shard_map/gather | solution.py:56
  (23 shorter events, 1.0 us)
Async XLA Ops:
  7.2 143.6 %all-gather.3.cloned.1.call-start = ((), (), s32[]{:S(2)}) async-start(), calls=%async_computation.3 | async-start | bytes 7864320 | tf_op jit(solution)/shard_map/all_gather | solution.py:46
  82.0 3.8 %copy-start.2 = (s32[384]{0:T(512)S(1)}, s32[384]{0:T(512)}, u32[]{:S(2)}) copy-start(s32[384]{0:T(512)} %param.8) | copy-start | bytes 4612
  82.0 13.3 %copy-start.1 = (s32[1,1536]{1,0:T(1,128)S(1)}, s32[1,1536]{1,0:T(1,128)}, u32[]{:S(2)}) copy-start(s32[1,1536]{1,0:T(1,128)} %param.9) | copy-start | bytes 18436
  82.0 13.4 %copy-start = (bf16[1536,1024]{1,0:T(8,128)(2,1)S(1)}, bf16[1536,1024]{1,0:T(8,128)(2,1)}, u32[]{:S(2)}) copy-start(bf16[1536,1024]{1,0:T(8,128)(2,1)} %param.5) | copy-start | bytes 9437188
  89.5 15.1 %all-to-all-start = ((bf16[64,12,1]{1,2,0:T(2,128)(2,1)}), bf16[64,12,1]{1,2,0:T(2,128)(2,1)S(1)}, u32[]{:S(2)}, u32[]{:S(2)}) async-start(bf16[64,12,1]{1,2,0:T(2,128)(2,1)} %all_to_all.33), calls=%async_computation | async-start | bytes 65536 | tf_op jit(solution)/shard_map/all_to_all | solution.py:41
  176.6 23.9 %all-to-all-start.2 = ((f32[64,12,1]{1,2,0:T(1,128)}), f32[64,12,1]{1,2,0:T(1,128)S(1)}, u32[]{:S(2)}, u32[]{:S(2)}) async-start(f32[64,12,1]{1,2,0:T(1,128)} %bitcast.1), calls=%async_computation.2 | async-start | bytes 65536 | tf_op jit(solution)/shard_map/all_to_all | solution.py:55
Sparse Core Ops, SparseCore 0:
  85.9 64.7 all-gather.2
where the time goes:
time: 212 us
  blocking collectives  86.5 us (41%)
  waiting for transfers between devices  52.5 us (25%)
  starting transfers between devices  20.4 us (10%)
  local copies, waits for them, and re-layouts  14.6 us (7%)
  between operations  14.2 us (7%)
  matrix products  13.4 us (6%)
  other arithmetic  10.1 us (5%)
    all_to_all x1, blocking collectives, shards(): lax.all_to_all(outgoing, 'ex', split_axis=0, concat_axis=0, tiled=True)  64.3 us
    all_gather x1, waiting for transfers between devices, shards(): lax.all_gather(arrived, 'rep', axis=0, tiled=True)  35.3 us
    all_to_all x1, starting transfers between devices, shards(): lax.all_to_all(row_best, 'ex', split_axis=0, concat_axis=0, tiled=True)  14.6 us
    dot_general x1, matrix products, tile_scores(): lax.dot_general(query_part, member_part, (((1,), (1,)), ((), ())), prefer...  13.4 us
    pmax x1, blocking collectives, shards(): row_all = lax.pmax(row_all, 'rep')  11.6 us
    all_gather x1, blocking collectives, shards(): lax.all_gather(arrived_labels, 'rep', axis=0, tiled=True)  10.5 us
    all_to_all x1, waiting for transfers between devices, shards(): lax.all_to_all(row_best, 'ex', split_axis=0, concat_axis=0, tiled=True)  8.68 us
    all_to_all x1, waiting for transfers between devices, shards(): lax.all_to_all(out_labels, 'ex', split_axis=0, concat_axis=0, tiled=True)  8.52 us
  transfers between devices with their start and end apart: 3, of which 3 were waited for; matrix products, arithmetic and copies ran while one was open for 2% of the time, Pallas kernels for 0%

commit v1 on v0

v1 whole, which is shorter than its diff:
```python
import functools

import jax
import jax.numpy as jnp
import numpy as np
from jax import lax
from jax.experimental import pallas as pl
from jax.experimental.pallas import tpu as pltpu
from jax.sharding import PartitionSpec as P

MESH = pl.DeviceIdType.MESH
F32, BF16 = jnp.float32, jnp.bfloat16
EXACT = lax.Precision.HIGHEST
CAP = 12
PIECES = 6
TILE = 512


def layout_tables():
    spread = np.zeros((192, 192), np.float32)
    for r in range(192):
        a, k, s = r // 48, (r % 48) // CAP, r % CAP
        spread[r, k * 48 + a * CAP + s] = 1
    member_of = np.zeros((96, 8), np.float32)
    lane_of = np.zeros((96, 128), np.float32)
    for r in range(96):
        member_of[r, r // CAP] = 1
        lane_of[r, r % CAP] = 1
    return spread, spread.T.copy(), member_of, member_of.T.copy(), lane_of


def unit_length(block):
    wide = block.astype(F32)
    squares = jnp.sum(wide * wide, axis=1, keepdims=True)
    return (wide * lax.rsqrt(squares + 1e-06)).astype(BF16)


def dot(a, b, contract, precision=None):
    return lax.dot_general(a, b, ((contract[:1], contract[1:]), ((), ())), preferred_element_type=F32, precision=precision)


def kernel(
    emb_ref, rows_ref, owner_ref, qcl_ref, mcl_ref, spread_ref, gather_ref, memb_ref, membt_ref, lane_ref,
    qmax_ref, rmax_ref,
    out, arrive, lab_out, lab_in, q_own, q_par, lab_own, lab_par, ql_own, ql_par, m_own, m_par, ml_own, ml_par,
    rm_own, rm_par, b_send, b_got, c_own, c_par, c_got, ret_out, ret_in,
    load_sem, s_sem, r_sem, ls_sem, lr_sem, f_s, f_r, fl_s, fl_r, m_s, m_r, ml_s, ml_r, b_s, b_r, c_s, c_r, t_s, t_r,
):
    ex, rep = lax.axis_index("ex"), lax.axis_index("rep")
    core, z, y = ex % 2, (ex // 2) % 8, ex // 16
    near = rep + 1 - 2 * (rep % 2)
    m_mate = (1 - core) * near + core * (3 - rep)
    q_mate = (1 - core) * (3 - rep) + core * near

    def shift(j):
        i = j // 8
        dz = (i % 2) * ((i + 1) // 2) + (1 - i % 2) * ((8 - i // 2) % 8)
        return (j // 2) % 4, dz, j % 2

    def target(j):
        dy, dz, dc = shift(j)
        return ((((y + dy) % 4) * 8 + (z + dz) % 8) * 2 + (core + dc) % 2, rep)

    def origin(j):
        dy, dz, dc = shift(j)
        return ((((y + 4 - dy) % 4) * 8 + (z + 8 - dz) % 8) * 2 + (core + 2 - dc) % 2, rep)

    barrier = pltpu.get_barrier_semaphore()

    def greet(j, carry):
        pl.semaphore_signal(barrier, inc=1, device_id=target(j), device_id_type=MESH)
        return carry

    for mate in (m_mate, q_mate):
        pl.semaphore_signal(barrier, inc=1, device_id=(ex, mate), device_id_type=MESH)
    lax.fori_loop(1, 64, greet, 0)

    piece = m_own.shape[0] // PIECES
    load = pltpu.make_async_copy(emb_ref, m_own, load_sem)
    load.start()

    owners = owner_ref[...]
    dz = ((owners >> 1) - z) & 7
    order = jnp.where(dz == 0, 0, jnp.where(dz <= 4, 2 * dz - 1, 16 - 2 * dz))
    dest = order * 8 + (((owners >> 4) - y) & 3) * 2 + ((owners - core) & 1)
    count = owners.shape[1]
    is_dest = jnp.where(lax.broadcasted_iota(jnp.int32, (64, count), 0) == dest, 1.0, 0.0)
    earlier = jnp.where(
        lax.broadcasted_iota(jnp.int32, (count, count), 0) < lax.broadcasted_iota(jnp.int32, (count, count), 1), 1.0, 0.0
    ).astype(BF16)
    before = dot(is_dest.astype(BF16), earlier, (1, 0))
    rank = jnp.sum(is_dest * before, axis=0, keepdims=True).astype(jnp.int32)
    slot = dest * CAP + rank
    is_rank = jnp.where(lax.broadcasted_iota(jnp.int32, (128, count), 0) == rank, 1.0, 0.0)
    labels = (qcl_ref[...] + 1).astype(F32)
    lab_out[...] = dot((is_dest * labels).astype(BF16), is_rank.astype(BF16), (1, 1)).reshape(64, 1, 128)
    queries = unit_length(rows_ref[...])

    def place(g, carry):
        pick = jnp.where(lax.broadcasted_iota(jnp.int32, (48, count), 0) + g * 48 == slot, 1.0, 0.0).astype(BF16)
        rows = dot(pick, queries, (1, 0)).astype(BF16)
        stacked = jnp.concatenate([rows[:, k * 256 : (k + 1) * 256] for k in range(4)], axis=0)
        spread = dot(spread_ref[...], stacked, (1, 0)).astype(BF16)
        for a in range(4):
            out[g * 4 + a] = spread[a * 48 : (a + 1) * 48]
        return carry

    lax.fori_loop(0, 16, place, 0)

    load.wait()

    def normalize(p, carry):
        part = pl.ds(pl.multiple_of(p * 64, 64), 64)
        m_own[part, :] = unit_length(m_own[part, :])
        return carry

    lax.fori_loop(0, m_own.shape[0] // 64, normalize, 0)
    ml_own[...] = (mcl_ref[...] + 1).astype(F32)

    pl.semaphore_wait(barrier, 65)

    def member_copy(p):
        part = pl.ds(pl.multiple_of(p * piece, 64), piece)
        return pltpu.make_async_remote_copy(
            m_own.at[part], m_par.at[part], m_s.at[p], m_r.at[p], device_id=(ex, m_mate), device_id_type=MESH
        )

    def member_label_copy():
        return pltpu.make_async_remote_copy(ml_own, ml_par, ml_s, ml_r, device_id=(ex, m_mate), device_id_type=MESH)

    def send(j):
        return pltpu.make_async_remote_copy(
            out.at[j], arrive.at[j], s_sem.at[j // 8], r_sem.at[j // 8], device_id=target(j), device_id_type=MESH
        )

    def send_label(j):
        return pltpu.make_async_remote_copy(
            lab_out.at[j], lab_in.at[j], ls_sem.at[j // 8], lr_sem.at[j // 8], device_id=target(j), device_id_type=MESH
        )

    def forward(i):
        part = pl.ds(pl.multiple_of(i * 96, 96), 96)
        return pltpu.make_async_remote_copy(
            q_own.at[part], q_par.at[part], f_s.at[i], f_r.at[i], device_id=(ex, q_mate), device_id_type=MESH
        )

    def forward_label(i):
        part = pl.ds(pl.multiple_of(i * 8, 8), 8)
        return pltpu.make_async_remote_copy(
            lab_own.at[part], lab_par.at[part], fl_s.at[i], fl_r.at[i], device_id=(ex, q_mate), device_id_type=MESH
        )

    def start_members(p, carry):
        member_copy(p).start()
        return carry

    lax.fori_loop(0, PIECES, start_members, 0)
    member_label_copy().start()

    def start_send(j, carry):
        send(j).start()
        send_label(j).start()
        return carry

    lax.fori_loop(1, 64, start_send, 0)
    arrive[0] = out[0]
    lab_in[0] = lab_out[0]

    def settle(ref, sem, i, first):
        part = ref.at[pl.ds(i * 8 + first, 8 - first)]
        pltpu.make_async_copy(part, part, sem.at[i]).wait()

    def label_column(block):
        spread = dot(memb_ref[...], block.astype(BF16), (1, 0))
        return jnp.sum(spread * lane_ref[...], axis=1, keepdims=True)

    def take(i, first):
        settle(arrive, r_sem, i, first)
        settle(lab_in, lr_sem, i, first)
        for h in range(2):
            block = arrive[pl.ds(i * 8 + h * 4, 4)].reshape(192, 256)
            rows = dot(gather_ref[...], block, (1, 0)).astype(BF16)
            part = pl.ds(pl.multiple_of(i * 96 + h * 48, 48), 48)
            for k in range(4):
                q_own[part, k * 256 : (k + 1) * 256] = rows[k * 48 : (k + 1) * 48]
        lab = lab_in[pl.ds(i * 8, 8)].reshape(8, 128)
        lab_own[pl.ds(pl.multiple_of(i * 8, 8), 8), :] = lab
        forward(i).start()
        forward_label(i).start()
        ql_own[pl.ds(pl.multiple_of(i * 96, 96), 96), :] = label_column(lab)

    def take_next(i, carry):
        take(i, 0)
        return carry

    def take_forward(i, carry):
        forward(i).wait_recv()
        forward_label(i).wait_recv()
        lab = lab_par[pl.ds(pl.multiple_of(i * 8, 8), 8), :]
        ql_par[pl.ds(pl.multiple_of(i * 96, 96), 96), :] = label_column(lab)
        return carry

    c_own[...] = jnp.full(c_own.shape, -1.0, F32)
    c_par[...] = jnp.full(c_par.shape, -1.0, F32)
    rm_own[...] = jnp.full(rm_own.shape, -1.0, F32)
    rm_par[...] = jnp.full(rm_par.shape, -1.0, F32)

    def score(q_ref, ql_ref, row_ref, m_ref, ml_ref, col_ref, first, rows):
        labels = ql_ref[first : first + rows, :]
        part = q_ref[first : first + rows, :]

        def tile(t, best):
            at = pl.ds(pl.multiple_of(t * TILE, TILE), TILE)
            cosine = dot(part, m_ref[at, :], (1, 1))
            cosine = jnp.where(labels == ml_ref[:, at], cosine, -1.0)
            col_ref[:, at] = jnp.maximum(col_ref[:, at], jnp.max(cosine, axis=0, keepdims=True))
            for k in range(TILE // 128):
                best = jnp.maximum(best, cosine[:, k * 128 : (k + 1) * 128])
            return best

        best = lax.fori_loop(0, m_ref.shape[0] // TILE, tile, jnp.full((rows, 128), -1.0, F32))
        row_ref[first : first + rows, :] = jnp.maximum(row_ref[first : first + rows, :], jnp.max(best, axis=1, keepdims=True))

    def row_block(row_ref, i):
        column = row_ref[pl.ds(pl.multiple_of(i * 96, 96), 96), :] * lane_ref[...]
        return dot(membt_ref[...], column, (1, 0), EXACT)

    take(0, 1)
    lax.fori_loop(1, 4, take_next, 0)
    score(q_own, ql_own, rm_own, m_own, ml_own, c_own, 0, 384)
    lax.fori_loop(4, 8, take_next, 0)
    score(q_own, ql_own, rm_own, m_own, ml_own, c_own, 384, 384)
    lax.fori_loop(0, 4, take_forward, 0)
    score(q_par, ql_par, rm_par, m_own, ml_own, c_own, 0, 384)

    def take_members(p, carry):
        member_copy(p).wait_recv()
        return carry

    lax.fori_loop(0, PIECES, take_members, 0)
    member_label_copy().wait_recv()
    score(q_par, ql_par, rm_par, m_par, ml_par, c_par, 0, 384)

    def trade(i):
        part = pl.ds(pl.multiple_of(i * 8, 8), 8)
        return pltpu.make_async_remote_copy(
            b_send.at[part], b_got.at[part], b_s.at[i], b_r.at[i], device_id=(ex, q_mate), device_id_type=MESH
        )

    def start_trade(i, carry):
        b_send[pl.ds(pl.multiple_of(i * 8, 8), 8), :] = row_block(rm_par, i)
        trade(i).start()
        return carry

    lax.fori_loop(0, 4, start_trade, 0)
    score(q_own, ql_own, rm_own, m_par, ml_par, c_par, 0, 384)
    score(q_own, ql_own, rm_own, m_par, ml_par, c_par, 384, 384)
    lax.fori_loop(4, 8, take_forward, 0)
    score(q_par, ql_par, rm_par, m_own, ml_own, c_own, 384, 384)
    score(q_par, ql_par, rm_par, m_par, ml_par, c_par, 384, 384)
    lax.fori_loop(4, 8, start_trade, 0)
    columns = pltpu.make_async_remote_copy(c_par, c_got, c_s, c_r, device_id=(ex, m_mate), device_id_type=MESH)
    columns.start()

    def answer(j):
        return pltpu.make_async_remote_copy(ret_out.at[j], ret_in.at[j], t_s, t_r, device_id=origin(j), device_id_type=MESH)

    def merge(i, carry):
        trade(i).wait_recv()
        best = jnp.maximum(row_block(rm_own, i), b_got[pl.ds(pl.multiple_of(i * 8, 8), 8), :])
        ret_out[pl.ds(i * 8, 8)] = best.reshape(8, 1, 128)
        return carry

    lax.fori_loop(0, 8, merge, 0)

    def start_answer(j, carry):
        answer(j).start()
        return carry

    lax.fori_loop(1, 64, start_answer, 0)
    ret_in[0] = ret_out[0]
    columns.wait()
    rmax_ref[...] = jnp.maximum(c_own[...], c_got[...])

    for i in range(8):
        first = 1 if i == 0 else 0
        settle(out, s_sem, i, first)
        settle(lab_out, ls_sem, i, first)
        forward(i).wait_send()
        forward_label(i).wait_send()
        trade(i).wait_send()
    for p in range(PIECES):
        member_copy(p).wait_send()
    member_label_copy().wait_send()

    answers = ret_in.at[pl.ds(1, 63)]
    pltpu.make_async_copy(answers, answers, t_r).wait()
    sent = ret_out.at[pl.ds(1, 63)]
    pltpu.make_async_copy(sent, sent, t_s).wait()
    by_rank = dot(ret_in[...].reshape(64, 128), is_dest, (0, 0), EXACT)
    qmax_ref[...] = jnp.sum(by_rank * is_rank, axis=0, keepdims=True)


def shards(embeddings, block_rows, owners, query_cluster, member_cluster):
    members, width = embeddings.shape
    count = block_rows.shape[0]
    spread, gather, member_of, member_of_t, lane_of = layout_tables()
    vmem = pl.BlockSpec(memory_space=pltpu.VMEM)
    dma = pltpu.SemaphoreType.DMA
    query_max, resident_max = pl.pallas_call(
        kernel,
        out_shape=(jax.ShapeDtypeStruct((1, count), F32), jax.ShapeDtypeStruct((1, members), F32)),
        in_specs=[pl.BlockSpec(memory_space=pl.ANY)] + [vmem] * 9,
        out_specs=(vmem, vmem),
        scratch_shapes=[
            pltpu.VMEM((64, 48, 256), BF16),
            pltpu.VMEM((64, 48, 256), BF16),
            pltpu.VMEM((64, 1, 128), F32),
            pltpu.VMEM((64, 1, 128), F32),
            pltpu.VMEM((768, width), BF16),
            pltpu.VMEM((768, width), BF16),
            pltpu.VMEM((64, 128), F32),
            pltpu.VMEM((64, 128), F32),
            pltpu.VMEM((768, 1), F32),
            pltpu.VMEM((768, 1), F32),
            pltpu.VMEM((members, width), BF16),
            pltpu.VMEM((members, width), BF16),
            pltpu.VMEM((1, members), F32),
            pltpu.VMEM((1, members), F32),
            pltpu.VMEM((768, 1), F32),
            pltpu.VMEM((768, 1), F32),
            pltpu.VMEM((64, 128), F32),
            pltpu.VMEM((64, 128), F32),
            pltpu.VMEM((1, members), F32),
            pltpu.VMEM((1, members), F32),
            pltpu.VMEM((1, members), F32),
            pltpu.VMEM((64, 1, 128), F32),
            pltpu.VMEM((64, 1, 128), F32),
            dma,
            dma((8,)), dma((8,)), dma((8,)), dma((8,)),
            dma((8,)), dma((8,)), dma((8,)), dma((8,)),
            dma((PIECES,)), dma((PIECES,)), dma, dma,
            dma((8,)), dma((8,)), dma, dma, dma, dma,
        ],
        compiler_params=pltpu.CompilerParams(collective_id=0, has_side_effects=True, vmem_limit_bytes=48 << 20),
    )(
        embeddings,
        block_rows,
        owners.reshape(1, count),
        query_cluster.reshape(1, count),
        member_cluster,
        jnp.asarray(spread, BF16),
        jnp.asarray(gather, BF16),
        jnp.asarray(member_of, BF16),
        jnp.asarray(member_of_t, F32),
        jnp.asarray(lane_of, F32),
    )
    return query_max.reshape(count), resident_max.reshape(members)


def solution(mesh):
    placed = (
        P(("ex", "rep"), None),
        P(("ex", "rep"), None),
        P(("ex", "rep"), None),
        P(("ex", "rep")),
        P("ex", "rep"),
    )
    return jax.shard_map(
        shards,
        mesh=mesh,
        in_specs=placed,
        out_specs=(P(("ex", "rep")), P(("ex", "rep"))),
        check_vma=False,
    )
```

time: 212 us -> 110 us (0.52)
  Pallas kernels: 0 us -> 99.2 us
  blocking collectives: 86.5 us -> 0 us
  waiting for transfers between devices: 52.5 us -> 0 us
  starting transfers between devices: 20.4 us -> 0 us
  between operations: 14.2 us -> 0.65 us
  matrix products: 13.4 us -> 0 us
  other arithmetic: 10.1 us -> 1.21 us
  local copies, waits for them, and re-layouts: 14.6 us -> 8.19 us
    pallas_call x0 -> x1, Pallas kernels: none -> 99.2 us  [shards(): pl.pallas_call(kernel, out_shape=(jax.ShapeDtypeStruct((1, count), F32),...]
    all_to_all x1 -> x0, blocking collectives: 64.3 us -> none  [shards(): lax.all_to_all(outgoing, 'ex', split_axis=0, concat_axis=0, tiled=True)]
    all_gather x1 -> x0, waiting for transfers between devices: 35.3 us -> none  [shards(): lax.all_gather(arrived, 'rep', axis=0, tiled=True)]
    all_to_all x2 -> x0, starting transfers between devices: 20.4 us -> none  [the longest x1 14.6 us: shards(): lax.all_to_all(row_best, 'ex', split_axis=0, concat_axis=0, tiled=True)]
    all_to_all x2 -> x0, waiting for transfers between devices: 17.2 us -> none  [the longest x1 8.68 us: shards(): lax.all_to_all(row_best, 'ex', split_axis=0, concat_axis=0, tiled=True)]
    dot_general x1 -> x0, matrix products: 13.4 us -> none  [tile_scores(): lax.dot_general(query_part, member_part, (((1,), (1,)), ((), ())), prefer...]
    pmax x1 -> x0, blocking collectives: 11.6 us -> none  [shards(): row_all = lax.pmax(row_all, 'rep')]
    all_gather x1 -> x0, blocking collectives: 10.5 us -> none  [shards(): lax.all_gather(arrived_labels, 'rep', axis=0, tiled=True)]
  transfers between devices with their start and end apart: 3 -> 0, of which waited for: 3 -> 0; matrix products, arithmetic and copies ran while one was open for 2% -> 0% of each run, Pallas kernels for 0% -> 0%
where the time goes in v1:
time: 110 us; the launch traced here: 109 us
  Pallas kernels  99.2 us (90%)
  local copies, waits for them, and re-layouts  8.19 us (7%)
  other arithmetic  1.21 us (1%)
    pallas_call x1, Pallas kernels, shards(): pl.pallas_call(kernel, out_shape=(jax.ShapeDtypeStruct((1, count), F32),...  99.2 us
    unnamed x16, local copies, waits for them, and re-layouts  7.51 us

profile of v1, /device:TPU:1, one launch (start us, length us, event | category | flops | bytes accessed | tf_op | source)
XLA Modules:
  0.0 109.2 jit_solution(17571413848555208517)
XLA Ops:
  0.6 0.7 reshape.17.qcl_ref
  1.3 0.0 copy-start
  1.3 1.9 %copy-done = bf16[1536,1024]{1,0:T(8,128)(2,1)S(1)} copy-done((bf16[1536,1024]{1,0:T(8,128)(2,1)S(1)}, bf16[1536,1024]{1,0:T(8,128)(2,1)}, u32[]{:S(2)}) %copy-start) | copy-done | bytes 3145752
  3.2 0.0 copy-start.1
  3.2 1.1 %copy-done.1 = bf16[384,1024]{1,0:T(8,128)(2,1)S(1)} copy-done((bf16[384,1024]{1,0:T(8,128)(2,1)S(1)}, bf16[384,1024]{1,0:T(8,128)(2,1)}, u32[]{:S(2)}) %copy-start.1) | copy-done | bytes 786456
  4.3 0.0 copy-start.2
  4.3 0.9 copy-done.2
  5.2 0.0 copy-start.3
  5.2 0.8 copy-done.3
  6.0 0.0 copy-start.4
  6.0 0.7 copy-done.4
  6.8 0.0 copy-start.5
  6.8 0.7 copy-done.5
  7.5 0.0 copy-start.6
  7.5 0.7 copy-done.6
  8.1 0.0 copy-start.7
  8.1 0.7 copy-done.7
  8.8 99.2 %shard_map.113 = (f32[1,384]{1,0:T(1,128)S(1)}, f32[1,1536]{1,0:T(1,128)S(1)}) custom-call(bf16[1536,1024]{1,0:T(8,128)(2,1)S(1)} %copy-done, bf16[384,1024]{1,0:T(8,128)(2,1)S(1)} %copy-done.1, s32[1,384]{1,0:T(1,128)S(1)} %bitcast.1, s32[1,384]{1,0:T(1,128)S(1)} %reshape.17.qcl_ref, s32[1,1536]{1,0:T(1,128)S(1)} %copy-done.5, ...), custom_call_target="tpu_custom_call" | custom-call | tf_op jit(solution)/shard_map/pallas_call | solution.py:310
  108.0 0.6 reduce.1
  108.6 0.6 reduce
Async XLA Ops:
  1.3 1.9 %copy-start = (bf16[1536,1024]{1,0:T(8,128)(2,1)S(1)}, bf16[1536,1024]{1,0:T(8,128)(2,1)}, u32[]{:S(2)}) copy-start(bf16[1536,1024]{1,0:T(8,128)(2,1)} %emb_ref.1) | copy-start | bytes 9437188
  3.2 1.1 %copy-start.1 = (bf16[384,1024]{1,0:T(8,128)(2,1)S(1)}, bf16[384,1024]{1,0:T(8,128)(2,1)}, u32[]{:S(2)}) copy-start(bf16[384,1024]{1,0:T(8,128)(2,1)} %rows_ref.1) | copy-start | bytes 2359300
  4.3 0.9 copy-start.2
  5.2 0.8 copy-start.3
  6.0 0.7 copy-start.4
  6.8 0.7 copy-start.5
  7.5 0.7 copy-start.6
  8.1 0.7 copy-start.7

commit v2 on v1

v2 whole, which is shorter than its diff:
```python
import jax
import jax.numpy as jnp
from jax import lax
from jax.experimental import pallas as pl
from jax.experimental.pallas import tpu as pltpu
from jax.sharding import PartitionSpec as P

MESH = pl.DeviceIdType.MESH
F32, BF16 = jnp.float32, jnp.bfloat16
EXACT = lax.Precision.HIGHEST
CAP = 12
PIECES = 6


def unit_length(block):
    wide = block.astype(F32)
    squares = jnp.sum(wide * wide, axis=1, keepdims=True)
    return (wide * lax.rsqrt(squares + 1e-06)).astype(BF16)


def dot(a, b, contract, precision=None):
    return lax.dot_general(a, b, ((contract[:1], contract[1:]), ((), ())), preferred_element_type=F32, precision=precision)


def iota(shape, axis):
    return lax.broadcasted_iota(jnp.int32, shape, axis)


def one_hot(match):
    return jnp.where(match, 1.0, 0.0)


def spread_index(r):
    a = (r * 1366) >> 16
    rest = r - a * 48
    k = (rest * 5462) >> 16
    return k * 48 + a * CAP + rest - k * CAP


def kernel(
    emb_ref, rows_ref, owner_ref, qcl_ref, mcl_ref,
    qmax_ref, rmax_ref,
    rows, owner, qcl, mcl, spread, gather,
    out, arrive, lab_out, lab_in, q_own, q_par, ql_own, ql_par, m_own, m_par, ml_own, ml_par, mlb_own, mlb_par,
    r_own, r_par, r_got, c_own, c_par, c_send, c_got, ret_out, ret_in,
    load_sem, s_sem, r_sem, ls_sem, lr_sem, f_s, f_r, fl_s, fl_r, m_s, m_r, ml_s, ml_r, b_s, b_r, c_s, c_r, t_s, t_r,
):
    ex, rep = lax.axis_index("ex"), lax.axis_index("rep")
    core, z, y = ex % 2, (ex // 2) % 8, ex // 16
    near = rep + 1 - 2 * (rep % 2)
    m_mate = (1 - core) * near + core * (3 - rep)
    q_mate = (1 - core) * (3 - rep) + core * near

    def shift(j):
        i = j // 8
        dz = (i % 2) * ((i + 1) // 2) + (1 - i % 2) * ((8 - i // 2) % 8)
        return (j // 2) % 4, dz, j % 2

    def target(j):
        dy, dz, dc = shift(j)
        return ((((y + dy) % 4) * 8 + (z + dz) % 8) * 2 + (core + dc) % 2, rep)

    def origin(j):
        dy, dz, dc = shift(j)
        return ((((y + 4 - dy) % 4) * 8 + (z + 8 - dz) % 8) * 2 + (core + 2 - dc) % 2, rep)

    barrier = pltpu.get_barrier_semaphore()

    def greet(j, carry):
        pl.semaphore_signal(barrier, inc=1, device_id=target(j), device_id_type=MESH)
        return carry

    for mate in (m_mate, q_mate):
        pl.semaphore_signal(barrier, inc=1, device_id=(ex, mate), device_id_type=MESH)

    piece = m_own.shape[0] // PIECES
    small = [
        pltpu.make_async_copy(source, target_ref, load_sem.at[k])
        for k, (source, target_ref) in enumerate(
            ((owner_ref, owner), (qcl_ref, qcl), (mcl_ref, mcl), (rows_ref, rows))
        )
    ]
    for copy in small:
        copy.start()

    def load(p):
        part = pl.ds(p * piece, piece)
        return pltpu.make_async_copy(emb_ref.at[part], m_own.at[part], load_sem.at[4 + p])

    for p in range(PIECES):
        load(p).start()
    lax.fori_loop(1, 64, greet, 0)

    spread[...] = one_hot(iota((192, 192), 1) == spread_index(iota((192, 192), 0))).astype(BF16)
    gather[...] = one_hot(iota((192, 192), 0) == spread_index(iota((192, 192), 1))).astype(BF16)

    small[0].wait()
    small[1].wait()
    owners = owner[...]
    count = owners.shape[1]
    dz = ((owners >> 1) - z) & 7
    order = jnp.where(dz == 0, 0, jnp.where(dz <= 4, 2 * dz - 1, 16 - 2 * dz))
    dest = order * 8 + (((owners >> 4) - y) & 3) * 2 + ((owners - core) & 1)
    is_dest = one_hot(iota((64, count), 0) == dest)
    earlier = one_hot(iota((count, count), 0) < iota((count, count), 1)).astype(BF16)
    before = dot(is_dest.astype(BF16), earlier, (1, 0))
    rank = jnp.sum(is_dest * before, axis=0, keepdims=True).astype(jnp.int32)
    slot = dest * CAP + rank
    lane = (dest & 7) * CAP + rank
    is_lane = one_hot(iota((128, count), 0) == lane)
    labels = (jnp.concatenate([qcl[k : k + 1, :] for k in range(count // 128)], axis=1) + 1).astype(F32)
    lab_out[...] = dot((is_dest * labels).astype(BF16), is_lane.astype(BF16), (1, 1)).reshape(64, 1, 128)
    small[3].wait()
    rows[...] = unit_length(rows[...])

    def normalize(p):
        load(p).wait()

        def some(t, carry):
            part = pl.ds(pl.multiple_of(p * piece + t * 64, 64), 64)
            m_own[part, :] = unit_length(m_own[part, :])
            return carry

        lax.fori_loop(0, piece // 64, some, 0)

    def member_copy(p):
        part = pl.ds(p * piece, piece)
        return pltpu.make_async_remote_copy(
            m_own.at[part], m_par.at[part], m_s.at[p], m_r.at[p], device_id=(ex, m_mate), device_id_type=MESH
        )

    def member_label_copy():
        return pltpu.make_async_remote_copy(ml_own, ml_par, ml_s, ml_r, device_id=(ex, m_mate), device_id_type=MESH)

    def send(j):
        return pltpu.make_async_remote_copy(
            out.at[j], arrive.at[j], s_sem.at[j // 8], r_sem.at[j // 8], device_id=target(j), device_id_type=MESH
        )

    def send_label(j):
        return pltpu.make_async_remote_copy(
            lab_out.at[j], lab_in.at[j], ls_sem.at[j // 8], lr_sem.at[j // 8], device_id=target(j), device_id_type=MESH
        )

    def forward(i):
        part = pl.ds(pl.multiple_of(i * 96, 96), 96)
        return pltpu.make_async_remote_copy(
            q_own.at[part], q_par.at[part], f_s.at[i], f_r.at[i], device_id=(ex, q_mate), device_id_type=MESH
        )

    def forward_labels(h):
        return pltpu.make_async_remote_copy(
            ql_own.at[h], ql_par.at[h], fl_s.at[h], fl_r.at[h], device_id=(ex, q_mate), device_id_type=MESH
        )

    small[2].wait()
    ml_own[...] = (mcl[...] + 1).astype(F32)
    normalize(0)
    pl.semaphore_wait(barrier, 65)
    member_label_copy().start()
    member_copy(0).start()

    def place(g):
        pick = one_hot(iota((192, count), 0) + g * 192 == slot).astype(BF16)
        placed = dot(pick, rows[...], (1, 0)).astype(BF16)
        for q in range(4):
            four = placed[q * 48 : (q + 1) * 48]
            stacked = jnp.concatenate([four[:, k * 256 : (k + 1) * 256] for k in range(4)], axis=0)
            laid = dot(spread[...], stacked, (1, 0)).astype(BF16)
            for a in range(4):
                out[g * 16 + q * 4 + a] = laid[a * 48 : (a + 1) * 48]

    def start_send(j, carry):
        send(j).start()
        send_label(j).start()
        return carry

    def place_next(g, carry):
        place(g)
        lax.fori_loop(g * 16, g * 16 + 16, start_send, 0)
        return carry

    place(0)
    lax.fori_loop(1, 16, start_send, 0)
    lax.fori_loop(1, 4, place_next, 0)
    arrive[0] = out[0]
    lab_in[0] = lab_out[0]
    for p in range(1, PIECES):
        normalize(p)
        member_copy(p).start()

    def widen(row_ref, wide_ref):
        for b in range(row_ref.shape[1] // 128):
            part = jnp.broadcast_to(row_ref[:, b * 128 : (b + 1) * 128], (128, 128))
            wide_ref[b * 128 : (b + 1) * 128, :] = part.T

    widen(ml_own, mlb_own)
    c_own[...] = jnp.full(c_own.shape, -1.0, F32)
    c_par[...] = jnp.full(c_par.shape, -1.0, F32)
    r_own[...] = jnp.full(r_own.shape, -1.0, F32)
    r_par[...] = jnp.full(r_par.shape, -1.0, F32)

    def settle(ref, sem, i, first):
        part = ref.at[pl.ds(i * 8 + first, 8 - first)]
        pltpu.make_async_copy(part, part, sem.at[i]).wait()

    def take(i, first):
        settle(arrive, r_sem, i, first)
        for h in range(2):
            block = arrive[pl.ds(i * 8 + h * 4, 4)].reshape(192, 256)
            back = dot(gather[...], block, (1, 0)).astype(BF16)
            part = pl.ds(pl.multiple_of(i * 96 + h * 48, 48), 48)
            for k in range(4):
                q_own[part, k * 256 : (k + 1) * 256] = back[k * 48 : (k + 1) * 48]
        forward(i).start()

    def take_next(i, carry):
        take(i, 0)
        return carry

    def take_labels(h):
        parts = []
        for i in range(h * 4, h * 4 + 4):
            settle(lab_in, lr_sem, i, 1 if i == 0 else 0)
            parts.append(jnp.sum(lab_in[i * 8 : i * 8 + 8], axis=0)[:, :96])
        ql_own[h] = jnp.concatenate(parts, axis=1)
        forward_labels(h).start()

    def take_forward(i, carry):
        forward(i).wait_recv()
        return carry

    def score(q_ref, ql_ref, row_ref, halves, m_ref, mlb_ref, col_ref, first, tiles):
        width = 384 * len(halves)
        start = 384 * halves[0]
        label_row = jnp.concatenate([ql_ref[h] for h in halves], axis=1)

        def tile(t, best):
            at = pl.ds(pl.multiple_of(first + t * 256, 256), 256)
            cosine = dot(m_ref[at, :], q_ref[start : start + width, :], (1, 1))
            wide = mlb_ref[at, :]
            column = col_ref[at, :]
            parts = []
            for k in range(width // 128):
                here = slice(k * 128, (k + 1) * 128)
                value = jnp.where(wide == label_row[:, here], cosine[:, here], -1.0)
                column = jnp.maximum(column, value)
                parts.append(jnp.max(value.reshape(32, 8, 128), axis=0))
            col_ref[at, :] = column
            return jnp.maximum(best, jnp.concatenate(parts, axis=1))

        best = lax.fori_loop(0, tiles, tile, jnp.full((8, width), -1.0, F32))
        there = slice(start, start + width)
        row_ref[:, there] = jnp.maximum(row_ref[:, there], jnp.max(best, axis=0, keepdims=True))

    own = m_own.shape[0] // 256
    take(0, 1)
    lax.fori_loop(1, 4, take_next, 0)
    take_labels(0)
    score(q_own, ql_own, r_own, (0,), m_own, mlb_own, c_own, 0, own)
    lax.fori_loop(4, 8, take_next, 0)
    take_labels(1)
    score(q_own, ql_own, r_own, (1,), m_own, mlb_own, c_own, 0, own)
    lax.fori_loop(0, 4, take_forward, 0)
    forward_labels(0).wait_recv()
    score(q_par, ql_par, r_par, (0,), m_own, mlb_own, c_own, 0, own)
    member_label_copy().wait_recv()
    widen(ml_par, mlb_par)
    lax.fori_loop(4, 8, take_forward, 0)
    forward_labels(1).wait_recv()
    score(q_par, ql_par, r_par, (1,), m_own, mlb_own, c_own, 0, own)
    for p in range(PIECES):
        member_copy(p).wait_recv()
        score(q_par, ql_par, r_par, (0, 1), m_par, mlb_par, c_par, p * piece, piece // 256)
        if p == PIECES - 1:
            trade = pltpu.make_async_remote_copy(r_par, r_got, b_s, b_r, device_id=(ex, q_mate), device_id_type=MESH)
            trade.start()
        score(q_own, ql_own, r_own, (0, 1), m_par, mlb_par, c_par, p * piece, piece // 256)

    def columns_of(col_ref, b):
        return jnp.max(col_ref[b * 128 : (b + 1) * 128, :].T, axis=0, keepdims=True)

    trade.wait_recv()
    merged = jnp.maximum(r_own[...], r_got[...])
    for i in range(8):
        ret_out[i] = jnp.concatenate([merged[:, i * 96 : (i + 1) * 96], jnp.zeros((1, 32), F32)], axis=1)

    def answer(j):
        return pltpu.make_async_remote_copy(
            ret_out.at[j // 8], ret_in.at[j], t_s, t_r, device_id=origin(j), device_id_type=MESH
        )

    def start_answer(j, carry):
        answer(j).start()
        return carry

    lax.fori_loop(1, 64, start_answer, 0)
    ret_in[0] = ret_out[0]
    blocks = c_par.shape[0] // 128
    for b in range(blocks):
        c_send[b : b + 1, :] = columns_of(c_par, b)
    columns = pltpu.make_async_remote_copy(c_send, c_got, c_s, c_r, device_id=(ex, m_mate), device_id_type=MESH)
    columns.start()
    for b in range(blocks):
        rmax_ref[b : b + 1, :] = columns_of(c_own, b)

    for i in range(8):
        first = 1 if i == 0 else 0
        settle(out, s_sem, i, first)
        settle(lab_out, ls_sem, i, first)
        forward(i).wait_send()
    for h in range(2):
        forward_labels(h).wait_send()
    for p in range(PIECES):
        member_copy(p).wait_send()
    member_label_copy().wait_send()
    trade.wait_send()

    answers = ret_in.at[pl.ds(1, 63)]
    pltpu.make_async_copy(answers, answers, t_s).wait()
    pltpu.make_async_copy(answers, answers, t_r).wait()
    by_lane = dot(ret_in[...].reshape(64, 128), is_dest, (0, 0), EXACT)
    result = jnp.sum(by_lane * is_lane, axis=0, keepdims=True)
    for k in range(count // 128):
        qmax_ref[k : k + 1, :] = result[:, k * 128 : (k + 1) * 128]
    columns.wait()
    rmax_ref[...] = jnp.maximum(rmax_ref[...], c_got[...])


def shards(embeddings, block_rows, owners, query_cluster, member_cluster):
    members, width = embeddings.shape
    count = block_rows.shape[0]
    vmem = pl.BlockSpec(memory_space=pltpu.VMEM)
    dma = pltpu.SemaphoreType.DMA
    v = pltpu.VMEM
    query_max, resident_max = pl.pallas_call(
        kernel,
        out_shape=(jax.ShapeDtypeStruct((count // 128, 128), F32), jax.ShapeDtypeStruct((members // 128, 128), F32)),
        in_specs=[pl.BlockSpec(memory_space=pl.ANY)] * 5,
        out_specs=(vmem, vmem),
        scratch_shapes=[
            v((count, width), BF16), v((1, count), jnp.int32), v((count // 128, 128), jnp.int32), v((1, members), jnp.int32),
            v((192, 192), BF16), v((192, 192), BF16),
            v((64, 48, 256), BF16), v((64, 48, 256), BF16), v((64, 1, 128), F32), v((64, 1, 128), F32),
            v((768, width), BF16), v((768, width), BF16), v((2, 1, 384), F32), v((2, 1, 384), F32),
            v((members, width), BF16), v((members, width), BF16), v((1, members), F32), v((1, members), F32),
            v((members, 128), F32), v((members, 128), F32),
            v((1, 768), F32), v((1, 768), F32), v((1, 768), F32),
            v((members, 128), F32), v((members, 128), F32), v((members // 128, 128), F32), v((members // 128, 128), F32),
            v((8, 1, 128), F32), v((64, 1, 128), F32),
            dma((4 + PIECES,)),
            dma((8,)), dma((8,)), dma((8,)), dma((8,)),
            dma((8,)), dma((8,)), dma((2,)), dma((2,)),
            dma((PIECES,)), dma((PIECES,)), dma, dma,
            dma, dma, dma, dma, dma, dma,
        ],
        compiler_params=pltpu.CompilerParams(collective_id=0, has_side_effects=True, vmem_limit_bytes=56 << 20),
    )(
        embeddings,
        block_rows,
        owners.reshape(1, count),
        query_cluster.reshape(count // 128, 128),
        member_cluster,
    )
    return query_max.reshape(count), resident_max.reshape(members)


def solution(mesh):
    placed = (
        P(("ex", "rep"), None),
        P(("ex", "rep"), None),
        P(("ex", "rep"), None),
        P(("ex", "rep")),
        P("ex", "rep"),
    )
    return jax.shard_map(
        shards,
        mesh=mesh,
        in_specs=placed,
        out_specs=(P(("ex", "rep")), P(("ex", "rep"))),
        check_vma=False,
    )
```

time: 110 us -> 89.5 us (0.81)
  Pallas kernels: 99.2 us -> 86.1 us
  local copies, waits for them, and re-layouts: 8.19 us -> 2.53 us
  other arithmetic: 1.21 us -> 0 us
    pallas_call x1, Pallas kernels: 99.2 us -> 86.1 us  [shards(): pl.pallas_call(kernel, out_shape=(jax.ShapeDtypeStruct((count // 128, 128...]
    unnamed x16 -> x2, local copies, waits for them, and re-layouts: 7.51 us -> 2.53 us
    pallas_call x2 -> x0, other arithmetic: 1.21 us -> none  [shards(): pl.pallas_call(kernel, out_shape=(jax.ShapeDtypeStruct((1, count), F32),...]
where the time goes in v2:
time: 89.5 us; the launch traced here: 89.3 us
  Pallas kernels  86.1 us (96%)
  local copies, waits for them, and re-layouts  2.53 us (3%)
    pallas_call x1, Pallas kernels, shards(): pl.pallas_call(kernel, out_shape=(jax.ShapeDtypeStruct((count // 128, 128...  86.1 us
    unnamed x2, local copies, waits for them, and re-layouts  2.53 us

profile of v2, /device:TPU:1, one launch (start us, length us, event | category | flops | bytes accessed | tf_op | source)
XLA Modules:
  0.0 89.3 jit_solution(17669824043844314974)
XLA Ops:
  0.6 86.1 %shard_map.68 = (f32[3,128]{1,0:T(4,128)}, f32[12,128]{1,0:T(8,128)}) custom-call(bf16[1536,1024]{1,0:T(8,128)(2,1)} %emb_ref.1, bf16[384,1024]{1,0:T(8,128)(2,1)} %rows_ref.1, s32[1,384]{1,0:T(1,128)} %bitcast.7, s32[3,128]{1,0:T(4,128)} %bitcast.5, s32[1,1536]{1,0:T(1,128)} %mcl_ref.1), custom_call_target="tpu_custom_call" | custom-call | tf_op jit(solution)/shard_map/pallas_call | solution.py:336
  86.8 1.2 %copy.9 = f32[384]{0:T(512)} copy(f32[384]{0:T(512)} %bitcast.6) | data formatting | bytes 3072
  88.0 1.3 %copy.10 = f32[1536]{0:T(1024)} copy(f32[1536]{0:T(1024)} %bitcast.4) | data formatting | bytes 12288

commit v3 on v2

--- a/solution.py
+++ b/solution.py
@@ -42,27 +42,29 @@
     qmax_ref, rmax_ref,
     rows, owner, qcl, mcl, spread, gather,
     out, arrive, lab_out, lab_in, q_own, q_par, ql_own, ql_par, m_own, m_par, ml_own, ml_par, mlb_own, mlb_par,
-    r_own, r_par, r_got, c_own, c_par, c_send, c_got, ret_out, ret_in,
-    load_sem, s_sem, r_sem, ls_sem, lr_sem, f_s, f_r, fl_s, fl_r, m_s, m_r, ml_s, ml_r, b_s, b_r, c_s, c_r, t_s, t_r,
+    r_own, r_par, r_got, c_own, c_par, c_send, c_got, ret_out, ret_mid, ret_in,
+    load_sem, s_sem, r_sem, ls_sem, lr_sem, f_s, f_r, fl_s, fl_r, m_s, m_r, ml_s, ml_r, b_s, b_r, c_s, c_r, tz_s, tz_r, t_s, t_r,
 ):
     ex, rep = lax.axis_index("ex"), lax.axis_index("rep")
-    core, z, y = ex % 2, (ex // 2) % 8, ex // 16
-    near = rep + 1 - 2 * (rep % 2)
+    core, z, y = lax.rem(ex, 2), lax.rem(lax.div(ex, 2), 8), lax.div(ex, 16)
+    near = rep + 1 - 2 * lax.rem(rep, 2)
     m_mate = (1 - core) * near + core * (3 - rep)
     q_mate = (1 - core) * (3 - rep) + core * near
 
+    def place_at(dy, dz, dc):
+        return ((lax.rem(y + dy, 4) * 8 + lax.rem(z + dz, 8)) * 2 + lax.rem(core + dc, 2), rep)
+
     def shift(j):
-        i = j // 8
-        dz = (i % 2) * ((i + 1) // 2) + (1 - i % 2) * ((8 - i // 2) % 8)
-        return (j // 2) % 4, dz, j % 2
+        if isinstance(j, int):
+            i = j // 8
+            return (j // 2) % 4, ((i + 1) // 2 if i % 2 else (8 - i // 2) % 8), j % 2
+        i = lax.div(j, 8)
+        odd = lax.rem(i, 2)
+        half = lax.div(i + 1, 2)
+        return lax.rem(lax.div(j, 2), 4), odd * half + (1 - odd) * lax.rem(8 - half, 8), lax.rem(j, 2)
 
     def target(j):
-        dy, dz, dc = shift(j)
-        return ((((y + dy) % 4) * 8 + (z + dz) % 8) * 2 + (core + dc) % 2, rep)
-
-    def origin(j):
-        dy, dz, dc = shift(j)
-        return ((((y + 4 - dy) % 4) * 8 + (z + 8 - dz) % 8) * 2 + (core + 2 - dc) % 2, rep)
+        return place_at(*shift(j))
 
     barrier = pltpu.get_barrier_semaphore()
 
@@ -134,12 +136,12 @@
 
     def send(j):
         return pltpu.make_async_remote_copy(
-            out.at[j], arrive.at[j], s_sem.at[j // 8], r_sem.at[j // 8], device_id=target(j), device_id_type=MESH
+            out.at[j], arrive.at[j], s_sem.at[lax.div(j, 8)], r_sem.at[lax.div(j, 8)], device_id=target(j), device_id_type=MESH
         )
 
     def send_label(j):
         return pltpu.make_async_remote_copy(
-            lab_out.at[j], lab_in.at[j], ls_sem.at[j // 8], lr_sem.at[j // 8], device_id=target(j), device_id_type=MESH
+            lab_out.at[j], lab_in.at[j], ls_sem.at[lax.div(j, 8)], lr_sem.at[lax.div(j, 8)], device_id=target(j), device_id_type=MESH
         )
 
     def forward(i):
@@ -218,6 +220,7 @@
         take(i, 0)
         return carry
 
+
     def take_labels(h):
         parts = []
         for i in range(h * 4, h * 4 + 4):
@@ -230,79 +233,105 @@
         forward(i).wait_recv()
         return carry
 
-    def score(q_ref, ql_ref, row_ref, halves, m_ref, mlb_ref, col_ref, first, tiles):
-        width = 384 * len(halves)
-        start = 384 * halves[0]
-        label_row = jnp.concatenate([ql_ref[h] for h in halves], axis=1)
+    def score(q_ref, ql_ref, row_ref, chunks, m_ref, mlb_ref, col_ref, first, rows):
+        width, start = 96 * len(chunks), 96 * chunks[0]
+        step = min(rows, 512)
+        label_row = jnp.concatenate([ql_ref[h] for h in range(chunks[0] // 4, chunks[-1] // 4 + 1)], axis=1)
 
         def tile(t, best):
-            at = pl.ds(pl.multiple_of(first + t * 256, 256), 256)
+            at = pl.ds(pl.multiple_of(first + t * step, 256), step)
             cosine = dot(m_ref[at, :], q_ref[start : start + width, :], (1, 1))
             wide = mlb_ref[at, :]
-            column = col_ref[at, :]
             parts = []
-            for k in range(width // 128):
-                here = slice(k * 128, (k + 1) * 128)
-                value = jnp.where(wide == label_row[:, here], cosine[:, here], -1.0)
-                column = jnp.maximum(column, value)
-                parts.append(jnp.max(value.reshape(32, 8, 128), axis=0))
-            col_ref[at, :] = column
+            for k in range(0, width, 128):
+                n = min(128, width - k)
+                value = jnp.where(wide[:, :n] == label_row[:, k : k + n], cosine[:, k : k + n], -1.0)
+                col_ref[at, :n] = jnp.maximum(col_ref[at, :n], value)
+                parts.append(jnp.max(value.reshape(step // 8, 8, n), axis=0))
             return jnp.maximum(best, jnp.concatenate(parts, axis=1))
 
-        best = lax.fori_loop(0, tiles, tile, jnp.full((8, width), -1.0, F32))
-        there = slice(start, start + width)
-        row_ref[:, there] = jnp.maximum(row_ref[:, there], jnp.max(best, axis=0, keepdims=True))
-
-    own = m_own.shape[0] // 256
+        best = lax.fori_loop(0, rows // step, tile, jnp.full((8, width), -1.0, F32))
+        best = jnp.max(best, axis=0, keepdims=True)
+        for k, i in enumerate(chunks):
+            row_ref[i, :, :96] = jnp.maximum(row_ref[i, :, :96], best[:, k * 96 : (k + 1) * 96])
+
+    members = m_own.shape[0]
+    whole, low, high = range(8), range(4), range(4, 8)
+
+    def score_own(q_ref, ql_ref, row_ref, chunks):
+        score(q_ref, ql_ref, row_ref, chunks, m_own, mlb_own, c_own, 0, members)
+
+    def score_pieces(q_ref, ql_ref, row_ref, chunks, first, last):
+        score(q_ref, ql_ref, row_ref, chunks, m_par, mlb_par, c_par, first * piece, (last - first) * piece)
+
+    def members_in(first, last):
+        for p in range(first, last):
+            member_copy(p).wait_recv()
+
     take(0, 1)
     lax.fori_loop(1, 4, take_next, 0)
     take_labels(0)
-    score(q_own, ql_own, r_own, (0,), m_own, mlb_own, c_own, 0, own)
-    lax.fori_loop(4, 8, take_next, 0)
-    take_labels(1)
-    score(q_own, ql_own, r_own, (1,), m_own, mlb_own, c_own, 0, own)
-    lax.fori_loop(0, 4, take_forward, 0)
-    forward_labels(0).wait_recv()
-    score(q_par, ql_par, r_par, (0,), m_own, mlb_own, c_own, 0, own)
+    score_own(q_own, ql_own, r_own, low)
+    take(4, 0)
     member_label_copy().wait_recv()
     widen(ml_par, mlb_par)
+    forward_labels(0).wait_recv()
+    take(5, 0)
+    lax.fori_loop(0, 4, take_forward, 0)
+    score_own(q_par, ql_par, r_par, low)
+    take(6, 0)
+    members_in(0, 2)
+    score_pieces(q_own, ql_own, r_own, low, 0, 2)
+    score_pieces(q_par, ql_par, r_par, low, 0, 2)
+    take(7, 0)
+    take_labels(1)
+    score_own(q_own, ql_own, r_own, high)
+    score_pieces(q_own, ql_own, r_own, high, 0, 2)
+    members_in(2, 4)
+    score_pieces(q_own, ql_own, r_own, whole, 2, 4)
+    score_pieces(q_par, ql_par, r_par, low, 2, 4)
+    forward_labels(1).wait_recv()
     lax.fori_loop(4, 8, take_forward, 0)
-    forward_labels(1).wait_recv()
-    score(q_par, ql_par, r_par, (1,), m_own, mlb_own, c_own, 0, own)
-    for p in range(PIECES):
-        member_copy(p).wait_recv()
-        score(q_par, ql_par, r_par, (0, 1), m_par, mlb_par, c_par, p * piece, piece // 256)
+    score_own(q_par, ql_par, r_par, high)
+    score_pieces(q_par, ql_par, r_par, high, 0, 4)
+    for p in range(4, PIECES):
+        members_in(p, p + 1)
+        score_pieces(q_par, ql_par, r_par, whole, p, p + 1)
         if p == PIECES - 1:
             trade = pltpu.make_async_remote_copy(r_par, r_got, b_s, b_r, device_id=(ex, q_mate), device_id_type=MESH)
             trade.start()
-        score(q_own, ql_own, r_own, (0, 1), m_par, mlb_par, c_par, p * piece, piece // 256)
+        score_pieces(q_own, ql_own, r_own, whole, p, p + 1)
 
     def columns_of(col_ref, b):
         return jnp.max(col_ref[b * 128 : (b + 1) * 128, :].T, axis=0, keepdims=True)
 
+    def answer_z(i):
+        return pltpu.make_async_remote_copy(
+            ret_out.at[i], ret_mid.at[i], tz_s.at[i], tz_r, device_id=place_at(0, 8 - shift(8 * i)[1], 0), device_id_type=MESH
+        )
+
+    def answer_y(k):
+        return pltpu.make_async_remote_copy(
+            ret_mid, ret_in.at[k], t_s.at[k], t_r, device_id=place_at(4 - k // 2, 0, 2 - k % 2), device_id_type=MESH
+        )
+
     trade.wait_recv()
-    merged = jnp.maximum(r_own[...], r_got[...])
-    for i in range(8):
-        ret_out[i] = jnp.concatenate([merged[:, i * 96 : (i + 1) * 96], jnp.zeros((1, 32), F32)], axis=1)
-
-    def answer(j):
-        return pltpu.make_async_remote_copy(
-            ret_out.at[j // 8], ret_in.at[j], t_s, t_r, device_id=origin(j), device_id_type=MESH
-        )
-
-    def start_answer(j, carry):
-        answer(j).start()
-        return carry
-
-    lax.fori_loop(1, 64, start_answer, 0)
-    ret_in[0] = ret_out[0]
-    blocks = c_par.shape[0] // 128
+    for i in range(1, 8):
+        ret_out[i] = jnp.maximum(r_own[i], r_got[i])
+        answer_z(i).start()
+    ret_mid[0] = jnp.maximum(r_own[0], r_got[0])
+    blocks = members // 128
     for b in range(blocks):
-        c_send[b : b + 1, :] = columns_of(c_par, b)
+        c_send[:, b * 128 : (b + 1) * 128] = columns_of(c_par, b)
     columns = pltpu.make_async_remote_copy(c_send, c_got, c_s, c_r, device_id=(ex, m_mate), device_id_type=MESH)
     columns.start()
+    far = ret_mid.at[pl.ds(1, 7)]
+    pltpu.make_async_copy(far, far, tz_r).wait()
+    for k in range(1, 8):
+        answer_y(k).start()
+    ret_in[0] = ret_mid[...]
     for b in range(blocks):
-        rmax_ref[b : b + 1, :] = columns_of(c_own, b)
+        rmax_ref[:, b * 128 : (b + 1) * 128] = columns_of(c_own, b)
 
     for i in range(8):
         first = 1 if i == 0 else 0
@@ -311,18 +340,19 @@
         forward(i).wait_send()
     for h in range(2):
         forward_labels(h).wait_send()
+    member_label_copy().wait_send()
     for p in range(PIECES):
         member_copy(p).wait_send()
-    member_label_copy().wait_send()
     trade.wait_send()
 
-    answers = ret_in.at[pl.ds(1, 63)]
-    pltpu.make_async_copy(answers, answers, t_s).wait()
+    for k in range(1, 8):
+        answer_z(k).wait_send()
+        answer_y(k).wait_send()
+    answers = ret_in.at[pl.ds(1, 7)]
     pltpu.make_async_copy(answers, answers, t_r).wait()
-    by_lane = dot(ret_in[...].reshape(64, 128), is_dest, (0, 0), EXACT)
-    result = jnp.sum(by_lane * is_lane, axis=0, keepdims=True)
-    for k in range(count // 128):
-        qmax_ref[k : k + 1, :] = result[:, k * 128 : (k + 1) * 128]
+    by_row = one_hot(iota((64, count), 0) == (dest & 7) * 8 + (dest >> 3))
+    by_lane = dot(ret_in[...].reshape(64, 128), by_row, (0, 0), EXACT)
+    qmax_ref[...] = jnp.sum(by_lane * is_lane, axis=0, keepdims=True)
     columns.wait()
     rmax_ref[...] = jnp.maximum(rmax_ref[...], c_got[...])
 
@@ -335,7 +365,7 @@
     v = pltpu.VMEM
     query_max, resident_max = pl.pallas_call(
         kernel,
-        out_shape=(jax.ShapeDtypeStruct((count // 128, 128), F32), jax.ShapeDtypeStruct((members // 128, 128), F32)),
+        out_shape=(jax.ShapeDtypeStruct((1, count), F32), jax.ShapeDtypeStruct((1, members), F32)),
         in_specs=[pl.BlockSpec(memory_space=pl.ANY)] * 5,
         out_specs=(vmem, vmem),
         scratch_shapes=[
@@ -345,14 +375,14 @@
             v((768, width), BF16), v((768, width), BF16), v((2, 1, 384), F32), v((2, 1, 384), F32),
             v((members, width), BF16), v((members, width), BF16), v((1, members), F32), v((1, members), F32),
             v((members, 128), F32), v((members, 128), F32),
-            v((1, 768), F32), v((1, 768), F32), v((1, 768), F32),
-            v((members, 128), F32), v((members, 128), F32), v((members // 128, 128), F32), v((members // 128, 128), F32),
-            v((8, 1, 128), F32), v((64, 1, 128), F32),
+            v((8, 1, 128), F32), v((8, 1, 128), F32), v((8, 1, 128), F32),
+            v((members, 128), F32), v((members, 128), F32), v((1, members), F32), v((1, members), F32),
+            v((8, 1, 128), F32), v((8, 1, 128), F32), v((8, 8, 1, 128), F32),
             dma((4 + PIECES,)),
             dma((8,)), dma((8,)), dma((8,)), dma((8,)),
             dma((8,)), dma((8,)), dma((2,)), dma((2,)),
             dma((PIECES,)), dma((PIECES,)), dma, dma,
-            dma, dma, dma, dma, dma, dma,
+            dma, dma, dma, dma, dma((8,)), dma, dma((8,)), dma,
         ],
         compiler_params=pltpu.CompilerParams(collective_id=0, has_side_effects=True, vmem_limit_bytes=56 << 20),
     )(

time: 89.5 us -> 86.1 us (0.962)
  Pallas kernels: 86.1 us -> 82.7 us
  other arithmetic: 0 us -> 2.58 us
  local copies, waits for them, and re-layouts: 2.53 us -> 0 us
    pallas_call x1, Pallas kernels: 86.1 us -> 82.7 us  [shards(): pl.pallas_call(kernel, out_shape=(jax.ShapeDtypeStruct((1, count), F32),...]
    pallas_call x0 -> x2, other arithmetic: none -> 2.58 us  [shards(): pl.pallas_call(kernel, out_shape=(jax.ShapeDtypeStruct((1, count), F32),...]
    unnamed x2 -> x0, local copies, waits for them, and re-layouts: 2.53 us -> none
where the time goes in v3:
time: 86.1 us; the launch traced here: 85.9 us
  Pallas kernels  82.7 us (96%)
  other arithmetic  2.58 us (3%)
    pallas_call x1, Pallas kernels, shards(): pl.pallas_call(kernel, out_shape=(jax.ShapeDtypeStruct((1, count), F32),...  82.7 us
    pallas_call x2, other arithmetic, shards(): pl.pallas_call(kernel, out_shape=(jax.ShapeDtypeStruct((1, count), F32),...  2.58 us

profile of v3, /device:TPU:1, one launch (start us, length us, event | category | flops | bytes accessed | tf_op | source)
XLA Modules:
  0.0 85.9 jit_solution(14998867605307571858)
XLA Ops:
  0.6 82.7 %shard_map.68 = (f32[1,384]{1,0:T(1,128)}, f32[1,1536]{1,0:T(1,128)}) custom-call(bf16[1536,1024]{1,0:T(8,128)(2,1)} %emb_ref.1, bf16[384,1024]{1,0:T(8,128)(2,1)} %rows_ref.1, s32[1,384]{1,0:T(1,128)} %bitcast.3, s32[3,128]{1,0:T(4,128)} %bitcast.2, s32[1,1536]{1,0:T(1,128)} %mcl_ref.1), custom_call_target="tpu_custom_call" | custom-call | tf_op jit(solution)/shard_map/pallas_call | solution.py:366
  83.3 1.3 %reduce.1 = f32[1536]{0:T(1024)} reduce(f32[1,1536]{1,0:T(1,128)} %get-tuple-element.5, f32[]{:T(128)} %constant.4), dimensions={0}, to_apply=%get-tuple-element.5.reduce_sub_computation | reduce | bytes 12292 | tf_op jit(solution)/shard_map/pallas_call | solution.py:366
  84.7 1.3 %reduce = f32[384]{0:T(512)} reduce(f32[1,384]{1,0:T(1,128)} %get-tuple-element.4, f32[]{:T(128)} %constant.4), dimensions={0}, to_apply=%get-tuple-element.4.reduce_sub_computation | reduce | bytes 3076 | tf_op jit(solution)/shard_map/pallas_call | solution.py:366

commit v4 on v3

--- a/solution.py
+++ b/solution.py
@@ -189,7 +189,8 @@
     lab_in[0] = lab_out[0]
     for p in range(1, PIECES):
         normalize(p)
-        member_copy(p).start()
+        if p < 5:
+            member_copy(p).start()
 
     def widen(row_ref, wide_ref):
         for b in range(row_ref.shape[1] // 128):
@@ -286,6 +287,8 @@
     take(7, 0)
     take_labels(1)
     score_own(q_own, ql_own, r_own, high)
+    forward(6).wait_send()
+    member_copy(5).start()
     score_pieces(q_own, ql_own, r_own, high, 0, 2)
     members_in(2, 4)
     score_pieces(q_own, ql_own, r_own, whole, 2, 4)
@@ -337,7 +340,8 @@
         first = 1 if i == 0 else 0
         settle(out, s_sem, i, first)
         settle(lab_out, ls_sem, i, first)
-        forward(i).wait_send()
+        if i != 6:
+            forward(i).wait_send()
     for h in range(2):
         forward_labels(h).wait_send()
     member_label_copy().wait_send()
@@ -365,7 +369,7 @@
     v = pltpu.VMEM
     query_max, resident_max = pl.pallas_call(
         kernel,
-        out_shape=(jax.ShapeDtypeStruct((1, count), F32), jax.ShapeDtypeStruct((1, members), F32)),
+        out_shape=(pltpu.VMEM((1, count), F32), pltpu.VMEM((1, members), F32)),
         in_specs=[pl.BlockSpec(memory_space=pl.ANY)] * 5,
         out_specs=(vmem, vmem),
         scratch_shapes=[

time: 86.1 us -> 80.8 us (0.938)
  Pallas kernels: 82.7 us -> 78.9 us
  other arithmetic: 2.58 us -> 1.21 us
    pallas_call x1, Pallas kernels: 82.7 us -> 78.9 us  [shards(): pl.pallas_call(kernel, out_shape=(pltpu.VMEM((1, count), F32), pltpu.VMEM...]
    pallas_call x2, other arithmetic: 2.58 us -> 1.21 us  [shards(): pl.pallas_call(kernel, out_shape=(pltpu.VMEM((1, count), F32), pltpu.VMEM...]
where the time goes in v4:
time: 80.8 us; the launch traced here: 80.7 us
  Pallas kernels  78.9 us (98%)
  other arithmetic  1.21 us (1%)
    pallas_call x1, Pallas kernels, shards(): pl.pallas_call(kernel, out_shape=(pltpu.VMEM((1, count), F32), pltpu.VMEM...  78.9 us

profile of v4, /device:TPU:1, one launch (start us, length us, event | category | flops | bytes accessed | tf_op | source)
XLA Modules:
  0.0 80.7 jit_solution(2487611829893802332)
XLA Ops:
  0.6 78.9 %shard_map.68 = (f32[1,384]{1,0:T(1,128)S(1)}, f32[1,1536]{1,0:T(1,128)S(1)}) custom-call(bf16[1536,1024]{1,0:T(8,128)(2,1)} %emb_ref.1, bf16[384,1024]{1,0:T(8,128)(2,1)} %rows_ref.1, s32[1,384]{1,0:T(1,128)} %bitcast.3, s32[3,128]{1,0:T(4,128)} %bitcast.2, s32[1,1536]{1,0:T(1,128)} %mcl_ref.1), custom_call_target="tpu_custom_call" | custom-call | tf_op jit(solution)/shard_map/pallas_call | solution.py:370
  79.5 0.6 reduce.1
  80.1 0.6 reduce

commit v5 on v4

--- a/solution.py
+++ b/solution.py
@@ -42,7 +42,7 @@
     qmax_ref, rmax_ref,
     rows, owner, qcl, mcl, spread, gather,
     out, arrive, lab_out, lab_in, q_own, q_par, ql_own, ql_par, m_own, m_par, ml_own, ml_par, mlb_own, mlb_par,
-    r_own, r_par, r_got, c_own, c_par, c_send, c_got, ret_out, ret_mid, ret_in,
+    r_own, r_par, mid_own, mid_par, c_own, c_par, c_send, c_got, ret_mid, ret_in,
     load_sem, s_sem, r_sem, ls_sem, lr_sem, f_s, f_r, fl_s, fl_r, m_s, m_r, ml_s, ml_r, b_s, b_r, c_s, c_r, tz_s, tz_r, t_s, t_r,
 ):
     ex, rep = lax.axis_index("ex"), lax.axis_index("rep")
@@ -74,6 +74,8 @@
 
     for mate in (m_mate, q_mate):
         pl.semaphore_signal(barrier, inc=1, device_id=(ex, mate), device_id_type=MESH)
+    for k in range(1, 8):
+        pl.semaphore_signal(barrier, inc=1, device_id=(place_at(0, k, 0)[0], q_mate), device_id_type=MESH)
 
     piece = m_own.shape[0] // PIECES
     small = [
@@ -158,7 +160,7 @@
     small[2].wait()
     ml_own[...] = (mcl[...] + 1).astype(F32)
     normalize(0)
-    pl.semaphore_wait(barrier, 65)
+    pl.semaphore_wait(barrier, 72)
     member_label_copy().start()
     member_copy(0).start()
 
@@ -297,39 +299,45 @@
     lax.fori_loop(4, 8, take_forward, 0)
     score_own(q_par, ql_par, r_par, high)
     score_pieces(q_par, ql_par, r_par, high, 0, 4)
+    def answer_z(i):
+        return pltpu.make_async_remote_copy(
+            r_own.at[i], mid_own.at[i], tz_s.at[i], tz_r, device_id=place_at(0, 8 - shift(8 * i)[1], 0), device_id_type=MESH
+        )
+
+    def answer_x(i):
+        there = place_at(0, 8 - shift(8 * i)[1], 0)[0] if i else ex
+        return pltpu.make_async_remote_copy(
+            r_par.at[i], mid_par.at[i], b_s.at[i], b_r, device_id=(there, q_mate), device_id_type=MESH
+        )
+
+    def answer_y(k):
+        return pltpu.make_async_remote_copy(
+            ret_mid, ret_in.at[k], t_s.at[k], t_r, device_id=place_at(4 - k // 2, 0, 2 - k % 2), device_id_type=MESH
+        )
+
     for p in range(4, PIECES):
         members_in(p, p + 1)
         score_pieces(q_par, ql_par, r_par, whole, p, p + 1)
         if p == PIECES - 1:
-            trade = pltpu.make_async_remote_copy(r_par, r_got, b_s, b_r, device_id=(ex, q_mate), device_id_type=MESH)
-            trade.start()
+            for i in range(8):
+                answer_x(i).start()
         score_pieces(q_own, ql_own, r_own, whole, p, p + 1)
 
     def columns_of(col_ref, b):
         return jnp.max(col_ref[b * 128 : (b + 1) * 128, :].T, axis=0, keepdims=True)
 
-    def answer_z(i):
-        return pltpu.make_async_remote_copy(
-            ret_out.at[i], ret_mid.at[i], tz_s.at[i], tz_r, device_id=place_at(0, 8 - shift(8 * i)[1], 0), device_id_type=MESH
-        )
-
-    def answer_y(k):
-        return pltpu.make_async_remote_copy(
-            ret_mid, ret_in.at[k], t_s.at[k], t_r, device_id=place_at(4 - k // 2, 0, 2 - k % 2), device_id_type=MESH
-        )
-
-    trade.wait_recv()
     for i in range(1, 8):
-        ret_out[i] = jnp.maximum(r_own[i], r_got[i])
         answer_z(i).start()
-    ret_mid[0] = jnp.maximum(r_own[0], r_got[0])
+    mid_own[0] = r_own[0]
     blocks = members // 128
     for b in range(blocks):
         c_send[:, b * 128 : (b + 1) * 128] = columns_of(c_par, b)
     columns = pltpu.make_async_remote_copy(c_send, c_got, c_s, c_r, device_id=(ex, m_mate), device_id_type=MESH)
     columns.start()
-    far = ret_mid.at[pl.ds(1, 7)]
+    far = mid_own.at[pl.ds(1, 7)]
     pltpu.make_async_copy(far, far, tz_r).wait()
+    pltpu.make_async_copy(mid_par, mid_par, b_r).wait()
+    ret_mid[...] = jnp.maximum(mid_own[...], mid_par[...])
     for k in range(1, 8):
         answer_y(k).start()
     ret_in[0] = ret_mid[...]
@@ -347,7 +355,8 @@
     member_label_copy().wait_send()
     for p in range(PIECES):
         member_copy(p).wait_send()
-    trade.wait_send()
+    for i in range(8):
+        answer_x(i).wait_send()
 
     for k in range(1, 8):
         answer_z(k).wait_send()
@@ -379,14 +388,14 @@
             v((768, width), BF16), v((768, width), BF16), v((2, 1, 384), F32), v((2, 1, 384), F32),
             v((members, width), BF16), v((members, width), BF16), v((1, members), F32), v((1, members), F32),
             v((members, 128), F32), v((members, 128), F32),
-            v((8, 1, 128), F32), v((8, 1, 128), F32), v((8, 1, 128), F32),
+            v((8, 1, 128), F32), v((8, 1, 128), F32), v((8, 1, 128), F32), v((8, 1, 128), F32),
             v((members, 128), F32), v((members, 128), F32), v((1, members), F32), v((1, members), F32),
-            v((8, 1, 128), F32), v((8, 1, 128), F32), v((8, 8, 1, 128), F32),
+            v((8, 1, 128), F32), v((8, 8, 1, 128), F32),
             dma((4 + PIECES,)),
             dma((8,)), dma((8,)), dma((8,)), dma((8,)),
             dma((8,)), dma((8,)), dma((2,)), dma((2,)),
             dma((PIECES,)), dma((PIECES,)), dma, dma,
-            dma, dma, dma, dma, dma((8,)), dma, dma((8,)), dma,
+            dma((8,)), dma, dma, dma, dma((8,)), dma, dma((8,)), dma,
         ],
         compiler_params=pltpu.CompilerParams(collective_id=0, has_side_effects=True, vmem_limit_bytes=56 << 20),
     )(

time: 80.8 us -> 78.9 us (0.976)
  Pallas kernels: 78.9 us -> 77 us
    pallas_call x1, Pallas kernels: 78.9 us -> 77 us  [shards(): pl.pallas_call(kernel, out_shape=(pltpu.VMEM((1, count), F32), pltpu.VMEM...]
where the time goes in v5:
time: 78.9 us
  Pallas kernels  77 us (98%)
  other arithmetic  1.21 us (2%)
    pallas_call x1, Pallas kernels, shards(): pl.pallas_call(kernel, out_shape=(pltpu.VMEM((1, count), F32), pltpu.VMEM...  77 us

profile of v5, /device:TPU:1, one launch (start us, length us, event | category | flops | bytes accessed | tf_op | source)
XLA Modules:
  0.0 78.9 jit_solution(12478928330157369987)
XLA Ops:
  0.6 77.0 %shard_map.68 = (f32[1,384]{1,0:T(1,128)S(1)}, f32[1,1536]{1,0:T(1,128)S(1)}) custom-call(bf16[1536,1024]{1,0:T(8,128)(2,1)} %emb_ref.1, bf16[384,1024]{1,0:T(8,128)(2,1)} %rows_ref.1, s32[1,384]{1,0:T(1,128)} %bitcast.3, s32[3,128]{1,0:T(4,128)} %bitcast.2, s32[1,1536]{1,0:T(1,128)} %mcl_ref.1), custom_call_target="tpu_custom_call" | custom-call | tf_op jit(solution)/shard_map/pallas_call | solution.py:379
  77.6 0.6 reduce.1
  78.3 0.6 reduce

commit v6 on v5

--- a/solution.py
+++ b/solution.py
@@ -238,7 +238,7 @@
 
     def score(q_ref, ql_ref, row_ref, chunks, m_ref, mlb_ref, col_ref, first, rows):
         width, start = 96 * len(chunks), 96 * chunks[0]
-        step = min(rows, 512)
+        step = rows if width < 500 and rows <= 1024 else min(rows, 768 if rows == 1536 else 512)
         label_row = jnp.concatenate([ql_ref[h] for h in range(chunks[0] // 4, chunks[-1] // 4 + 1)], axis=1)
 
         def tile(t, best):
@@ -344,6 +344,11 @@
     for b in range(blocks):
         rmax_ref[:, b * 128 : (b + 1) * 128] = columns_of(c_own, b)
 
+    by_row = one_hot(iota((64, count), 0) == (dest & 7) * 8 + (dest >> 3))
+    answers = ret_in.at[pl.ds(1, 7)]
+    pltpu.make_async_copy(answers, answers, t_r).wait()
+    by_lane = dot(ret_in[...].reshape(64, 128), by_row, (0, 0), EXACT)
+    qmax_ref[...] = jnp.sum(by_lane * is_lane, axis=0, keepdims=True)
     for i in range(8):
         first = 1 if i == 0 else 0
         settle(out, s_sem, i, first)
@@ -361,11 +366,6 @@
     for k in range(1, 8):
         answer_z(k).wait_send()
         answer_y(k).wait_send()
-    answers = ret_in.at[pl.ds(1, 7)]
-    pltpu.make_async_copy(answers, answers, t_r).wait()
-    by_row = one_hot(iota((64, count), 0) == (dest & 7) * 8 + (dest >> 3))
-    by_lane = dot(ret_in[...].reshape(64, 128), by_row, (0, 0), EXACT)
-    qmax_ref[...] = jnp.sum(by_lane * is_lane, axis=0, keepdims=True)
     columns.wait()
     rmax_ref[...] = jnp.maximum(rmax_ref[...], c_got[...])
 

time: 78.9 us -> 78.9 us (level)
  no operation moved by 1% of the time
where the time goes in v6:
time: 78.9 us; the launch traced here: 78.8 us
  Pallas kernels  77 us (98%)
  other arithmetic  1.21 us (2%)
    pallas_call x1, Pallas kernels, shards(): pl.pallas_call(kernel, out_shape=(pltpu.VMEM((1, count), F32), pltpu.VMEM...  77 us

profile of v6, /device:TPU:1, one launch (start us, length us, event | category | flops | bytes accessed | tf_op | source)
XLA Modules:
  0.0 78.8 jit_solution(13838314220310236416)
XLA Ops:
  0.6 77.0 %shard_map.68 = (f32[1,384]{1,0:T(1,128)S(1)}, f32[1,1536]{1,0:T(1,128)S(1)}) custom-call(bf16[1536,1024]{1,0:T(8,128)(2,1)} %emb_ref.1, bf16[384,1024]{1,0:T(8,128)(2,1)} %rows_ref.1, s32[1,384]{1,0:T(1,128)} %bitcast.3, s32[3,128]{1,0:T(4,128)} %bitcast.2, s32[1,1536]{1,0:T(1,128)} %mcl_ref.1), custom_call_target="tpu_custom_call" | custom-call | tf_op jit(solution)/shard_map/pallas_call | solution.py:379
  77.6 0.6 reduce.1
  78.2 0.6 reduce
